TPU v7x, 32 devices: a whole 2x2x4 slice. The times are simulated.
32 devices in a mesh: pack: 2 (over y), gx: 4 (over z), gy: 4 (over x, core).
Axes of the slice: x: 2, y: 2, z: 4, core: 2. Of those that a mesh axis runs over, the one named last changes fastest.
Arguments:
- modes_in: float32 [32, 3, 64, 512], P(None, None, ('pack', 'gx'), 'gy'), parts along dimension 2, may hold values from -6 to 6
- dirs_in: float32 [32, 3, 64, 512], P(None, None, ('pack', 'gx'), 'gy'), parts along dimension 2, may hold values from -6 to 6
- onsite: float32 [3, 64, 512], P(None, ('pack', 'gx'), 'gy'), parts along dimension 1, may hold values from 0.3 to 10
- bond_terms: float32 [8, 4, 64, 512], P(None, None, ('pack', 'gx'), 'gy'), parts along dimension 2, as said below
- contacts: int32 [8, 64, 512], P(None, ('pack', 'gx'), 'gy'), parts along dimension 1, may hold values from 0 to 1, as said below
Outputs:
- modes: float32 [32, 3, 64, 512], P(None, None, ('pack', 'gx'), 'gy'), parts along dimension 2
- ritz_values: float32 [64], P('pack'), parts along dimension 0
There are 2 independent parts, one for each index of `pack`. A program takes and returns all parts, laid end to end along the dimension named above; each array names one. Nothing has to cross between parts.
Inputs may be any that keep to these rules, and one draw needn't show every extreme that they name: Contact lists are mutual: contacts[d + 4] at grain (x, y) equals contacts[d] at grain (x, y) - e_d, periodic, for d = 0..3 with e_0..e_3 = (1,0), (0,1), (1,1), (1,-1). bond_terms[d + 4] at grain (x, y) equals bond_terms[d] at grain (x, y) - e_d, periodic, for d = 0..3; bond_terms[d, 3] is positive.
All inputs are finite; a program needn't handle non-finite values.
Results may differ from a plain program's by a relative error of at most 0.0003.
Values sent between devices are 32-bit elements; how exact they have to be, the bound alone decides.
A program may use at most 64 MiB of HBM per device.

v0:
```python
import math

import jax
import jax.numpy as jnp
from jax import lax
from jax.sharding import PartitionSpec as P

ITERS = 2


highest = lax.Precision.HIGHEST
offsets = ((1, 0), (0, 1), (1, 1), (1, -1), (-1, 0), (0, -1), (-1, -1), (-1, 1))
third_turn = 2.0 * math.pi / 3.0


def with_halo(cells, sides, width):
    for axis, dim in sides:
        count = lax.axis_size(axis)
        head = lax.slice_in_dim(cells, 0, width, axis=dim)
        tail = lax.slice_in_dim(cells, cells.shape[dim] - width, cells.shape[dim], axis=dim)
        cells = jnp.concatenate(
            [
                lax.ppermute(tail, axis, [(i, (i + 1) % count) for i in range(count)]),
                cells,
                lax.ppermute(head, axis, [((i + 1) % count, i) for i in range(count)]),
            ],
            axis=dim,
        )
    return cells


def bond_coefs(bond_terms, contacts):
    contact_on = contacts.astype(jnp.float32)
    bond_vecs = bond_terms[:, 0:3] * contact_on[:, None]
    bond_soft = bond_terms[:, 3] * contact_on
    return (bond_vecs, bond_soft)


def stretch_terms(result, field, beside, bond_vecs, bond_soft, direction):
    stretch = field - beside
    along = jnp.sum(bond_vecs[direction][None] * stretch, axis=1, keepdims=True)
    return result + bond_vecs[direction][None] * along + bond_soft[direction][None, None] * stretch


def local_apply(padded, bond_vecs, bond_soft, onsite):
    extent_x, extent_y = (padded.shape[2] - 2, padded.shape[3] - 2)
    field = padded[:, :, 1 : 1 + extent_x, 1 : 1 + extent_y]
    result = onsite[None] * field
    for direction in range(8):
        step_x, step_y = offsets[direction]
        beside = padded[
            :, :, 1 + step_x : 1 + step_x + extent_x, 1 + step_y : 1 + step_y + extent_y
        ]
        result = stretch_terms(result, field, beside, bond_vecs, bond_soft, direction)
    return result


def apply_field(field, bond_vecs, bond_soft, onsite):
    padded = with_halo(field, (("gx", 2), ("gy", 3)), 1)
    return local_apply(padded, bond_vecs, bond_soft, onsite)


def three_images(current, search, coefs):
    bond_vecs, bond_soft, onsite = coefs
    mode_count = current.shape[0]
    paired = apply_field(jnp.concatenate([current, search], 0), bond_vecs, bond_soft, onsite)
    mode_image, search_image = (paired[:mode_count], paired[mode_count:])
    image_image = apply_field(mode_image, bond_vecs, bond_soft, onsite)
    return (mode_image, search_image, image_image)


def diag_blocks(matrix, mode_count):
    return jnp.diagonal(matrix.reshape(3, mode_count, 3, mode_count), axis1=1, axis2=3)


def pencil_lowest(gram_diag, hess_diag):
    gram_sym = 0.5 * (gram_diag + jnp.swapaxes(gram_diag, 0, 1))
    hess_sym = 0.5 * (hess_diag + jnp.swapaxes(hess_diag, 0, 1))
    empty_entry = jnp.zeros_like(gram_sym[0, 0])
    factor = [[empty_entry for j in range(3)] for i in range(3)]
    for i in range(3):
        for j in range(i + 1):
            pivot = gram_sym[i, j] - sum((factor[i][k] * factor[j][k] for k in range(j)))
            if i == j:
                factor[i][i] = jnp.sqrt(pivot)
            else:
                factor[i][j] = pivot / factor[j][j]
    inverse = [[empty_entry for j in range(3)] for i in range(3)]
    for j in range(3):
        inverse[j][j] = 1.0 / factor[j][j]
        for i in range(j + 1, 3):
            inverse[i][j] = -sum((factor[i][k] * inverse[k][j] for k in range(j, i))) / factor[i][i]
    inv_lower = jnp.stack([jnp.stack(row) for row in inverse])
    reduced = jnp.einsum("ijm,jkm,lkm->ilm", inv_lower, hess_sym, inv_lower, precision=highest)
    middle = (reduced[0, 0] + reduced[1, 1] + reduced[2, 2]) / 3.0
    identity = jnp.eye(3, dtype=jnp.float32)[:, :, None]
    centred = reduced - middle[None, None] * identity
    spread = jnp.sqrt(jnp.sum(centred * centred, axis=(0, 1)) / 6.0)
    determinant = (
        centred[0, 0] * (centred[1, 1] * centred[2, 2] - centred[1, 2] * centred[2, 1])
        - centred[0, 1] * (centred[1, 0] * centred[2, 2] - centred[1, 2] * centred[2, 0])
        + centred[0, 2] * (centred[1, 0] * centred[2, 1] - centred[1, 1] * centred[2, 0])
    )
    cosine = jnp.clip(determinant / (2.0 * spread * spread * spread), -1.0, 1.0)
    third_angle = jnp.arccos(cosine) / 3.0
    lowest = middle + 2.0 * spread * jnp.cos(third_angle + third_turn)
    pencil = hess_sym - lowest[None, None] * gram_sym
    vector = jnp.stack(
        [
            pencil[1, 1] * pencil[2, 2] - pencil[1, 2] * pencil[2, 1],
            pencil[1, 2] * pencil[2, 0] - pencil[1, 0] * pencil[2, 2],
            pencil[1, 0] * pencil[2, 1] - pencil[1, 1] * pencil[2, 0],
        ]
    )
    return (lowest, vector)


def coefficients(vector, gram_diag):
    raw_coef = jnp.concatenate(
        [jnp.diag(vector[0]), jnp.diag(vector[1]), jnp.diag(vector[2])], axis=0
    )
    dir_sq = (
        vector[1] * vector[1] * gram_diag[1, 1]
        + vector[1] * vector[2] * (gram_diag[1, 2] + gram_diag[2, 1])
        + vector[2] * vector[2] * gram_diag[2, 2]
    )
    dir_scale = 1.0 / jnp.sqrt(dir_sq + 1e-06)
    dir_coef = jnp.concatenate(
        [
            jnp.zeros_like(jnp.diag(vector[0])),
            jnp.diag(vector[1] * dir_scale),
            jnp.diag(vector[2] * dir_scale),
        ],
        axis=0,
    )
    return (raw_coef, dir_coef)


def body(modes_in, dirs_in, onsite, bond_terms, contacts):
    bond_vecs, bond_soft = bond_coefs(bond_terms, contacts)
    coefs = (bond_vecs, bond_soft, onsite)
    mode_count = modes_in.shape[0]
    grid_shape = modes_in.shape
    entries = 3 * modes_in.shape[2] * modes_in.shape[3] * lax.axis_size("gx") * lax.axis_size("gy")
    current, search = (modes_in, dirs_in)
    mode_image, search_image, image_image = three_images(current, search, coefs)
    lowest = jnp.zeros((mode_count,), jnp.float32)
    for sweep in range(ITERS):
        basis_rows = jnp.concatenate([current, mode_image, search], 0).reshape(3 * mode_count, -1)
        image_rows = jnp.concatenate([mode_image, image_image, search_image], 0).reshape(
            3 * mode_count, -1
        )
        gram, hess_gram = lax.psum(
            (
                jnp.dot(basis_rows, basis_rows.T, precision=highest),
                jnp.dot(basis_rows, image_rows.T, precision=highest),
            ),
            ("gx", "gy"),
        )
        gram = gram / entries
        hess_gram = hess_gram / entries
        gram_diag = diag_blocks(gram, mode_count)
        hess_diag = diag_blocks(hess_gram, mode_count)
        lowest, vector = pencil_lowest(gram_diag, hess_diag)
        raw_coef, dir_coef = coefficients(vector, gram_diag)
        mode_gram = jnp.dot(
            raw_coef.T, jnp.dot(gram, raw_coef, precision=highest), precision=highest
        )
        raw_rows = jnp.dot(raw_coef.T, basis_rows, precision=highest)
        chol_lower = jnp.linalg.cholesky(mode_gram)
        current = jax.scipy.linalg.solve_triangular(chol_lower, raw_rows, lower=True).reshape(
            grid_shape
        )
        search = jnp.dot(dir_coef.T, basis_rows, precision=highest).reshape(grid_shape)
        if sweep + 1 < ITERS:
            mode_image, search_image, image_image = three_images(current, search, coefs)
    return (current, lowest)


def solution(mesh):
    in_specs = (
        P(None, None, ("pack", "gx"), "gy"),
        P(None, None, ("pack", "gx"), "gy"),
        P(None, ("pack", "gx"), "gy"),
        P(None, None, ("pack", "gx"), "gy"),
        P(None, ("pack", "gx"), "gy"),
    )
    out_specs = (P(None, None, ("pack", "gx"), "gy"), P("pack"))
    return jax.shard_map(body, mesh=mesh, in_specs=in_specs, out_specs=out_specs, check_vma=False)
```

profile of v0, /device:TPU:0, one launch (start us, length us, event | category | flops | bytes accessed | tf_op | source)
XLA Modules:
  0.0 317.5 jit_solution(15524484297118186467)
XLA Ops:
  9.3 5.1 %collective-permute-start = (f32[64,3,1,128]{3,0,2,1:T(8,128)S(1)}, f32[64,3,1,128]{3,0,2,1:T(8,128)S(1)}, u32[]{:S(2)}, u32[]{:S(2)}) collective-permute-start(f32[64,3,1,128]{3,0,2,1:T(8,128)S(1)} %get-tuple-element.100), channel_id=1, source_target_pairs={{4,0},{8,4},{12,8},{0,12},{5,1},{9,5},{13,9},{1,13},{6,2},{10,6},{... | collective-permute-start | bytes 294920 | tf_op jit(solution)/shard_map/ppermute | solution.py:25
  14.6 2.9 collective-permute-done
  17.5 3.2 %collective-permute-done.1 = f32[64,3,1,128]{3,0,2,1:T(8,128)S(1)} collective-permute-done((f32[64,3,1,128]{3,0,2,1:T(8,128)S(1)}, f32[64,3,1,128]{3,0,2,1:T(8,128)S(1)}, u32[]{:S(2)}, u32[]{:S(2)}) %collective-permute-start.1) | collective-permute-done | bytes 98336 | tf_op jit(solution)/shard_map/ppermute | solution.py:23
  27.2 2.1 multiply_add_fusion.1
  33.4 2.8 collective-permute-done.5
  37.1 10.1 %collective-permute-done.6 = f32[32,3,10,1]{3,0,2,1:T(8,128)S(1)} collective-permute-done((f32[32,3,10,1]{3,0,2,1:T(8,128)S(1)}, f32[32,3,10,1]{3,0,2,1:T(8,128)S(1)}, u32[]{:S(2)}, u32[]{:S(2)}) %collective-permute-start.6) | collective-permute-done | bytes 3872 | tf_op jit(solution)/shard_map/ppermute | solution.py:25
  47.2 2.9 collective-permute-done.7
  55.2 83.4 %all-reduce.9.cloned.1.call-done = (f32[96,96]{1,0:T(8,128)}, f32[96,96]{1,0:T(8,128)}) async-done(((f32[96,96]{1,0:T(8,128)}, f32[96,96]{1,0:T(8,128)}), (f32[96,96]{1,0:T(8,128)}, f32[96,96]{1,0:T(8,128)})) %all-reduce.9.cloned.1.call-update) | async-done | bytes 73744 | tf_op jit(solution)/shard_map/psum | solution.py:153
  139.6 1.9 copy.151
  141.5 2.3 gather_fusion.1
  145.1 1.9 copy.149
  147.0 2.3 gather_fusion
  153.1 2.9 cholesky.44
  157.4 2.4 custom-call.14
  162.4 2.3 collective-permute-start.8
  164.8 2.3 collective-permute-done.8
  167.1 4.1 %collective-permute-done.9 = f32[64,3,1,128]{3,0,2,1:T(8,128)S(1)} collective-permute-done((f32[64,3,1,128]{3,0,2,1:T(8,128)S(1)}, f32[64,3,1,128]{3,0,2,1:T(8,128)S(1)}, u32[]{:S(2)}, u32[]{:S(2)}) %collective-permute-start.9) | collective-permute-done | bytes 98336 | tf_op jit(solution)/shard_map/ppermute | solution.py:23
  173.8 1.9 collective-permute-done.11
  178.5 2.0 multiply_add_fusion
  187.5 10.4 %collective-permute-done.14 = f32[32,3,10,1]{3,0,2,1:T(8,128)S(1)} collective-permute-done((f32[32,3,10,1]{3,0,2,1:T(8,128)S(1)}, f32[32,3,10,1]{3,0,2,1:T(8,128)S(1)}, u32[]{:S(2)}, u32[]{:S(2)}) %collective-permute-start.14) | collective-permute-done | bytes 3872 | tf_op jit(solution)/shard_map/ppermute | solution.py:25
  197.9 2.3 collective-permute-done.15
  204.3 84.4 %all-reduce.7.cloned.1.call-done = (f32[96,96]{1,0:T(8,128)}, f32[96,96]{1,0:T(8,128)}) async-done(((f32[96,96]{1,0:T(8,128)}, f32[96,96]{1,0:T(8,128)}), (f32[96,96]{1,0:T(8,128)}, f32[96,96]{1,0:T(8,128)})) %all-reduce.7.cloned.1.call-update) | async-done | bytes 73744 | tf_op jit(solution)/shard_map/psum | solution.py:153
  301.9 2.9 cholesky.55
  306.1 2.4 custom-call.15
  (267 shorter events, 60.7 us)
Async XLA Ops:
  7.2 131.4 %all-reduce.9.cloned.1.call-start = ((), (), s32[]{:S(2)}) async-start(), calls=%async_computation.1 | async-start | bytes 196608 | tf_op jit(solution)/shard_map/psum | solution.py:153
  9.3 8.3 %collective-permute-start = (f32[64,3,1,128]{3,0,2,1:T(8,128)S(1)}, f32[64,3,1,128]{3,0,2,1:T(8,128)S(1)}, u32[]{:S(2)}, u32[]{:S(2)}) collective-permute-start(f32[64,3,1,128]{3,0,2,1:T(8,128)S(1)} %get-tuple-element.100), channel_id=1, source_target_pairs={{4,0},{8,4},{12,8},{0,12},{5,1},{9,5},{13,9},{1,13},{6,2},{10,6},{... | collective-permute-start | bytes 294920 | tf_op jit(solution)/shard_map/ppermute | solution.py:25
  14.4 6.4 %collective-permute-start.1 = (f32[64,3,1,128]{3,0,2,1:T(8,128)S(1)}, f32[64,3,1,128]{3,0,2,1:T(8,128)S(1)}, u32[]{:S(2)}, u32[]{:S(2)}) collective-permute-start(f32[64,3,1,128]{3,0,2,1:T(8,128)S(1)} %get-tuple-element.99), channel_id=1, source_target_pairs={{0,4},{4,8},{8,12},{12,0},{1,5},{5,9},{9,13},{13,1},{2,6},{6,10},{... | collective-permute-start | bytes 294920 | tf_op jit(solution)/shard_map/ppermute | solution.py:23
  14.4 36.5 %copy-start.1 = (f32[3,8,128]{2,1,0:T(8,128)}, f32[3,8,128]{2,1,0:T(8,128)S(1)}, u32[]{:S(2)}) copy-start(f32[3,8,128]{2,1,0:T(8,128)S(1)} %get-tuple-element.120) | copy-start | bytes 36868
  14.5 36.5 %copy-start.3 = (f32[3,8,128]{2,1,0:T(8,128)}, f32[3,8,128]{2,1,0:T(8,128)S(1)}, u32[]{:S(2)}) copy-start(f32[3,8,128]{2,1,0:T(8,128)S(1)} %get-tuple-element.113) | copy-start | bytes 36868
  14.5 36.5 %copy-start.5 = (f32[3,8,128]{2,1,0:T(8,128)}, f32[3,8,128]{2,1,0:T(8,128)S(1)}, u32[]{:S(2)}) copy-start(f32[3,8,128]{2,1,0:T(8,128)S(1)} %get-tuple-element.114) | copy-start | bytes 36868
  14.5 36.5 %copy-start.7 = (f32[3,8,128]{2,1,0:T(8,128)}, f32[3,8,128]{2,1,0:T(8,128)S(1)}, u32[]{:S(2)}) copy-start(f32[3,8,128]{2,1,0:T(8,128)S(1)} %get-tuple-element.115) | copy-start | bytes 36868
  14.5 36.5 %copy-start.9 = (f32[3,8,128]{2,1,0:T(8,128)}, f32[3,8,128]{2,1,0:T(8,128)S(1)}, u32[]{:S(2)}) copy-start(f32[3,8,128]{2,1,0:T(8,128)S(1)} %get-tuple-element.116) | copy-start | bytes 36868
  21.6 1.5 collective-permute-start.2
  22.0 3.2 %collective-permute-start.3 = (f32[64,3,10,1]{0,3,2,1:T(1,128)S(1)}, f32[64,3,10,1]{0,3,2,1:T(1,128)S(1)}, u32[]{:S(2)}, u32[]{:S(2)}) collective-permute-start(f32[64,3,10,1]{0,3,2,1:T(1,128)S(1)} %copy.145), channel_id=1, source_target_pairs={{0,1},{1,2},{2,3},{3,0},{4,5},{5,6},{6,7},{7,4},{8,9},{9,10},{10,1... | collective-permute-start | bytes 23048 | tf_op jit(solution)/shard_map/ppermute | solution.py:23
  29.3 4.1 %collective-permute-start.4 = (f32[32,3,1,128]{3,0,2,1:T(8,128)S(1)}, f32[32,3,1,128]{3,0,2,1:T(8,128)S(1)}, u32[]{:S(2)}, u32[]{:S(2)}) collective-permute-start(f32[32,3,1,128]{3,0,2,1:T(8,128)S(1)} %get-tuple-element.98), channel_id=1, source_target_pairs={{4,0},{8,4},{12,8},{0,12},{5,1},{9,5},{13,9},{1,13},{6,2},{10,6},{... | collective-permute-start | bytes 147464 | tf_op jit(solution)/shard_map/ppermute | solution.py:25
  30.3 5.9 %collective-permute-start.5 = (f32[32,3,1,128]{3,0,2,1:T(8,128)S(1)}, f32[32,3,1,128]{3,0,2,1:T(8,128)S(1)}, u32[]{:S(2)}, u32[]{:S(2)}) collective-permute-start(f32[32,3,1,128]{3,0,2,1:T(8,128)S(1)} %get-tuple-element.97), channel_id=1, source_target_pairs={{0,4},{4,8},{8,12},{12,0},{1,5},{5,9},{9,13},{13,1},{2,6},{6,10},{... | collective-permute-start | bytes 147464 | tf_op jit(solution)/shard_map/ppermute | solution.py:23
  31.4 113.3 %copy-start.49 = (f32[3]{0:T(128)}, f32[3]{0:T(128)S(1)}, u32[]{:S(2)}) copy-start(f32[3]{0:T(128)S(1)} %pad.74.clone) | copy-start | bytes 40
  36.5 10.7 %collective-permute-start.6 = (f32[32,3,10,1]{3,0,2,1:T(8,128)S(1)}, f32[32,3,10,1]{3,0,2,1:T(8,128)S(1)}, u32[]{:S(2)}, u32[]{:S(2)}) collective-permute-start(f32[32,3,10,1]{3,0,2,1:T(8,128)S(1)} %get-tuple-element.108), channel_id=1, source_target_pairs={{1,0},{2,1},{3,2},{0,3},{5,4},{6,5},{7,6},{4,7},{9,8},{10,9},{11,1... | collective-permute-start | bytes 11528 | tf_op jit(solution)/shard_map/ppermute | solution.py:25
  36.5 13.6 %collective-permute-start.7 = (f32[32,3,10,1]{3,0,2,1:T(8,128)S(1)}, f32[32,3,10,1]{3,0,2,1:T(8,128)S(1)}, u32[]{:S(2)}, u32[]{:S(2)}) collective-permute-start(f32[32,3,10,1]{3,0,2,1:T(8,128)S(1)} %get-tuple-element.107), channel_id=1, source_target_pairs={{0,1},{1,2},{2,3},{3,0},{4,5},{5,6},{6,7},{7,4},{8,9},{9,10},{10,1... | collective-permute-start | bytes 11528 | tf_op jit(solution)/shard_map/ppermute | solution.py:23
  53.7 235.0 %all-reduce.7.cloned.1.call-start = ((), (), s32[]{:S(2)}) async-start(), calls=%async_computation | async-start | bytes 196608 | tf_op jit(solution)/shard_map/psum | solution.py:153
  162.4 4.7 %collective-permute-start.8 = (f32[64,3,1,128]{3,0,2,1:T(8,128)S(1)}, f32[64,3,1,128]{3,0,2,1:T(8,128)S(1)}, u32[]{:S(2)}, u32[]{:S(2)}) collective-permute-start(f32[64,3,1,128]{3,0,2,1:T(8,128)S(1)} %get-tuple-element.95), channel_id=1, source_target_pairs={{4,0},{8,4},{12,8},{0,12},{5,1},{9,5},{13,9},{1,13},{6,2},{10,6},{... | collective-permute-start | bytes 294920 | tf_op jit(solution)/shard_map/ppermute | solution.py:25
  164.8 6.4 %collective-permute-start.9 = (f32[64,3,1,128]{3,0,2,1:T(8,128)S(1)}, f32[64,3,1,128]{3,0,2,1:T(8,128)S(1)}, u32[]{:S(2)}, u32[]{:S(2)}) collective-permute-start(f32[64,3,1,128]{3,0,2,1:T(8,128)S(1)} %get-tuple-element.94), channel_id=1, source_target_pairs={{0,4},{4,8},{8,12},{12,0},{1,5},{5,9},{9,13},{13,1},{2,6},{6,10},{... | collective-permute-start | bytes 294920 | tf_op jit(solution)/shard_map/ppermute | solution.py:23
  172.0 1.5 collective-permute-start.10
  172.4 3.4 %collective-permute-start.11 = (f32[64,3,10,1]{0,3,2,1:T(1,128)S(1)}, f32[64,3,10,1]{0,3,2,1:T(1,128)S(1)}, u32[]{:S(2)}, u32[]{:S(2)}) collective-permute-start(f32[64,3,10,1]{0,3,2,1:T(1,128)S(1)} %copy.163), channel_id=1, source_target_pairs={{0,1},{1,2},{2,3},{3,0},{4,5},{5,6},{6,7},{7,4},{8,9},{9,10},{10,1... | collective-permute-start | bytes 23048 | tf_op jit(solution)/shard_map/ppermute | solution.py:23
  180.6 4.7 %collective-permute-start.12 = (f32[32,3,1,128]{3,0,2,1:T(8,128)S(1)}, f32[32,3,1,128]{3,0,2,1:T(8,128)S(1)}, u32[]{:S(2)}, u32[]{:S(2)}) collective-permute-start(f32[32,3,1,128]{3,0,2,1:T(8,128)S(1)} %get-tuple-element.93), channel_id=1, source_target_pairs={{4,0},{8,4},{12,8},{0,12},{5,1},{9,5},{13,9},{1,13},{6,2},{10,6},{... | collective-permute-start | bytes 147464 | tf_op jit(solution)/shard_map/ppermute | solution.py:25
  180.8 5.9 %collective-permute-start.13 = (f32[32,3,1,128]{3,0,2,1:T(8,128)S(1)}, f32[32,3,1,128]{3,0,2,1:T(8,128)S(1)}, u32[]{:S(2)}, u32[]{:S(2)}) collective-permute-start(f32[32,3,1,128]{3,0,2,1:T(8,128)S(1)} %get-tuple-element.92), channel_id=1, source_target_pairs={{0,4},{4,8},{8,12},{12,0},{1,5},{5,9},{9,13},{13,1},{2,6},{6,10},{... | collective-permute-start | bytes 147464 | tf_op jit(solution)/shard_map/ppermute | solution.py:23
  186.9 11.0 %collective-permute-start.14 = (f32[32,3,10,1]{3,0,2,1:T(8,128)S(1)}, f32[32,3,10,1]{3,0,2,1:T(8,128)S(1)}, u32[]{:S(2)}, u32[]{:S(2)}) collective-permute-start(f32[32,3,10,1]{3,0,2,1:T(8,128)S(1)} %get-tuple-element.104), channel_id=1, source_target_pairs={{1,0},{2,1},{3,2},{0,3},{5,4},{6,5},{7,6},{4,7},{9,8},{10,9},{11,1... | collective-permute-start | bytes 11528 | tf_op jit(solution)/shard_map/ppermute | solution.py:25
  187.0 13.3 %collective-permute-start.15 = (f32[32,3,10,1]{3,0,2,1:T(8,128)S(1)}, f32[32,3,10,1]{3,0,2,1:T(8,128)S(1)}, u32[]{:S(2)}, u32[]{:S(2)}) collective-permute-start(f32[32,3,10,1]{3,0,2,1:T(8,128)S(1)} %get-tuple-element.103), channel_id=1, source_target_pairs={{0,1},{1,2},{2,3},{3,0},{4,5},{5,6},{6,7},{7,4},{8,9},{9,10},{10,1... | collective-permute-start | bytes 11528 | tf_op jit(solution)/shard_map/ppermute | solution.py:23
  (45 other events, 236.9 us)
Sparse Core Ops, SparseCore 0:
  53.9 84.6 all-reduce.8
  203.8 84.8 all-reduce.6
where the time goes:
time: 318 us; the launch traced here: 317 us
  waiting for transfers between devices  215 us (68%)
  other arithmetic  32.9 us (10%)
  local copies, waits for them, and re-layouts  25.3 us (8%)
  between operations  15.4 us (5%)
  starting transfers between devices  14.3 us (4%)
  matrix products  14.2 us (4%)
    psum x2, waiting for transfers between devices, body(): lax.psum((jnp.dot(basis_rows, basis_rows.T, precision=highest), jnp.dot(b...  168 us
    ppermute x8, waiting for transfers between devices, with_halo(): lax.ppermute(head, axis, [((i + 1) % count, i) for i in range(count)])  27.1 us
    ppermute x8, waiting for transfers between devices, with_halo(): lax.ppermute(tail, axis, [(i, (i + 1) % count) for i in range(count)])  20.4 us
    ppermute x8, starting transfers between devices, with_halo(): lax.ppermute(head, axis, [((i + 1) % count, i) for i in range(count)])  8.86 us
    another operation x6, other arithmetic, body(): chol_lower = jnp.linalg.cholesky(mode_gram)  7.2 us
    gather x8, local copies, waits for them, and re-layouts, diag_blocks(): jnp.diagonal(matrix.reshape(3, mode_count, 3, mode_count), axis1=1, axis2=3)  7.07 us
  transfers between devices with their start and end apart: 18, of which 17 were waited for; matrix products, arithmetic and copies ran while one was open for 2% of the time, Pallas kernels for 0%

commit v1 on v0

v1 whole, which is shorter than its diff:
```python
import functools
import math

import numpy as np
import jax
import jax.numpy as jnp
from jax import lax
from jax.experimental import pallas as pl
from jax.experimental.pallas import tpu as pltpu
from jax.sharding import PartitionSpec as P

ITERS = 2
MESH = pl.DeviceIdType.MESH
highest = lax.Precision.HIGHEST
offsets = ((1, 0), (0, 1), (1, 1), (1, -1), (-1, 0), (0, -1), (-1, -1), (-1, 1))

CUR, SRCH, IMG, IIMG, SIMG, THIRD, SIIMG = (32 * i for i in range(7))


def lowest_root_poly():
    nodes = np.cos(np.pi * (np.arange(64) + 0.5) / 64)
    level = 0.5 * (nodes + 1.0)
    root = np.cos(2.0 * np.arcsin(level) / 3.0 + 2.0 * np.pi / 3.0)
    cheb = np.polynomial.chebyshev.chebfit(nodes, root, 11)
    return [float(c) for c in np.polynomial.chebyshev.cheb2poly(cheb)]


ROOT_POLY = lowest_root_poly()


def lanes(rows=8):
    return lax.broadcasted_iota(jnp.int32, (rows, 128), 1)


def pencil_lowest(g, h):
    f = [[None] * 3 for _ in range(3)]
    inv = [[None] * 3 for _ in range(3)]
    recip = [None] * 3
    for i in range(3):
        for j in range(i + 1):
            pivot = g[i][j]
            for k in range(j):
                pivot = pivot - f[i][k] * f[j][k]
            if i == j:
                f[i][i] = jnp.sqrt(pivot)
                recip[i] = 1.0 / f[i][i]
            else:
                f[i][j] = pivot * recip[j]
    for j in range(3):
        inv[j][j] = recip[j]
        for i in range(j + 1, 3):
            acc = f[i][j] * inv[j][j]
            for k in range(j + 1, i):
                acc = acc + f[i][k] * inv[k][j]
            inv[i][j] = -acc * recip[i]
    half = [[sum(inv[i][j] * h[j][k] for j in range(i + 1)) for k in range(3)] for i in range(3)]
    b = [[None] * 3 for _ in range(3)]
    for i in range(3):
        for l in range(i + 1):
            b[i][l] = b[l][i] = sum(half[i][k] * inv[l][k] for k in range(l + 1))
    middle = (b[0][0] + b[1][1] + b[2][2]) * (1.0 / 3.0)
    c00, c11, c22 = b[0][0] - middle, b[1][1] - middle, b[2][2] - middle
    c01, c02, c12 = b[0][1], b[0][2], b[1][2]
    total = c00 * c00 + c11 * c11 + c22 * c22 + 2.0 * (c01 * c01 + c02 * c02 + c12 * c12)
    spread = jnp.sqrt(total * (1.0 / 6.0))
    det = (
        c00 * (c11 * c22 - c12 * c12)
        - c01 * (c01 * c22 - c12 * c02)
        + c02 * (c01 * c12 - c11 * c02)
    )
    cosine = jnp.clip(det / (2.0 * spread * spread * spread), -1.0, 1.0)
    u = 2.0 * jnp.sqrt((1.0 - cosine) * 0.5) - 1.0
    t = jnp.full_like(u, ROOT_POLY[-1])
    for coef in ROOT_POLY[-2::-1]:
        t = t * u + coef
    lowest = middle + 2.0 * spread * t
    p = [[h[i][j] - lowest * g[i][j] for j in range(3)] for i in range(3)]
    vector = (
        p[1][1] * p[2][2] - p[1][2] * p[2][1],
        p[1][2] * p[2][0] - p[1][0] * p[2][2],
        p[1][0] * p[2][1] - p[1][1] * p[2][0],
    )
    return lowest, vector


def inverse_factor(sym):
    lane, row = lanes(32), lax.broadcasted_iota(jnp.int32, (32, 128), 0)
    aug = jnp.where(lane < 32, (lane == row).astype(jnp.float32), pltpu.roll(sym, 32, 1))
    blocks = [aug[8 * b : 8 * b + 8] for b in range(4)]
    sub = lax.broadcasted_iota(jnp.int32, (8, 128), 0)
    for j in range(32):
        home, at = j // 8, j % 8
        pivot_row = blocks[home][at : at + 1]
        scaled = pivot_row * (1.0 / pivot_row[:, 32 + j : 33 + j])
        for b in range(home, 4):
            if b == home and at == 7:
                continue
            step = blocks[b][:, 32 + j : 33 + j] * scaled
            if b == home:
                step = jnp.where(sub > at, step, 0.0)
            blocks[b] = blocks[b] - step
    aug = jnp.concatenate(blocks, 0)
    pivots = jnp.sum(jnp.where(lane == row + 32, aug, 0.0), 1, keepdims=True)
    return jnp.where(lane < 32, aug / jnp.sqrt(pivots), 0.0)


def small_step(top, low):
    lane, row = lanes(32), lax.broadcasted_iota(jnp.int32, (32, 128), 0)
    beside = lane == 96 + (row + 1) % 32

    def diag(x, off):
        return jnp.sum(jnp.where(lane == row + off, x, 0.0), 1, keepdims=True)

    cc, cp, ca, ab = (diag(top, 32 * i) for i in range(4))
    aa, pp, pa, pb = (diag(low, 32 * i) for i in range(4))
    pq = jnp.sum(jnp.where(beside, low, 0.0), 1, keepdims=True)
    g = [[cc, ca, cp], [ca, aa, pa], [cp, pa, pp]]
    h = [[ca, aa, pa], [aa, ab, pb], [pa, pb, pq]]
    lowest, (v0, v1, v2) = pencil_lowest(g, h)
    dir_sq = v1 * v1 * aa + 2.0 * (v1 * v2) * pa + v2 * v2 * pp
    dir_scale = 1.0 / jnp.sqrt(dir_sq + 1e-06)

    def across(a, b, c, d):
        pick = jnp.where(lane < 64, jnp.where(lane < 32, a, b), jnp.where(lane < 96, c, d))
        return jnp.sum(jnp.where(lane % 32 == row, pick, 0.0), 0, keepdims=True)

    zero = jnp.zeros_like(v0)
    part = top * v0 * across(0.5 * v0, v2, v1, zero)
    part = part + low * jnp.where(lane < 32, v1, v2) * across(0.5 * v1, 0.5 * v2, v1, zero)
    folded = part + pltpu.roll(part, 96, 1) + pltpu.roll(part, 64, 1)
    folded = jnp.where(lane < 32, folded, 0.0)
    square = jnp.concatenate([folded, jnp.zeros((96, 128), jnp.float32)], 0)
    sym = folded + square.T[:32]
    linv = inverse_factor(sym)
    four = linv + pltpu.roll(linv, 32, 1) + pltpu.roll(linv, 64, 1) + pltpu.roll(linv, 96, 1)
    mixes = (
        four * across(v0, v2, v1, zero),
        four * across(v0, v1, v2, zero),
        four * across(v0, zero, v1, v2),
    )
    low_row = jnp.sum(jnp.where(lane == row, lowest, 0.0), 0, keepdims=True)
    return low_row, mixes, v1 * dir_scale, v2 * dir_scale


def kernel(
    nx,
    ny,
    entries,
    modes_ref,
    dirs_ref,
    onsite_ref,
    bond_ref,
    contact_ref,
    out_ref,
    low_ref,
    basis,
    basis2,
    coef,
    pack,
    col_in,
    diag_in,
    row_in,
    slots_y,
    slots_x,
    halo_send,
    halo_recv,
    y_send,
    y_recv,
    x_send,
    x_recv,
):
    part, gx, gy = lax.axis_index("pack"), lax.axis_index("gx"), lax.axis_index("gy")

    def peer(dx, dy):
        return (part, lax.rem(gx + dx + nx, nx), lax.rem(gy + dy + ny, ny))

    diagonals = ((-1, -1), (-1, 1), (1, -1), (1, 1))
    peers = [peer(0, o) for o in range(1, ny)] + [peer(o, 0) for o in range(1, nx)]
    peers += [peer(*d) for d in diagonals]
    barrier = pltpu.get_barrier_semaphore()
    for device in peers:
        pl.semaphore_signal(barrier, inc=1, device_id=device, device_id_type=MESH)

    lane8 = lanes(8)

    def eight(block, base=0):
        return pl.ds(pl.multiple_of(base + 8 * block, 8), 8)

    for x in range(8):
        for c in range(3):
            basis[3 * x + c, CUR : CUR + 32] = modes_ref[pl.ds(8 * c + x, 32, stride=24), :]
            basis[3 * x + c, SRCH : SRCH + 32] = dirs_ref[pl.ds(8 * c + x, 32, stride=24), :]
    for d in range(8):
        on = contact_ref[d].astype(jnp.float32)
        for t in range(4):
            coef[4 * d + t] = bond_ref[d, t] * on
    for c in range(3):
        coef[32 + c] = onsite_ref[c]

    def pack_edges(e, fields):
        def block(b, carry):
            first = jnp.zeros((8, 128), jnp.float32)
            last = jnp.zeros((8, 128), jnp.float32)
            for f, base in enumerate(fields):
                for q in range(24):
                    lane = 32 * f + q
                    u = basis[q, eight(b, base), :]
                    at_lane = lane8 == lane
                    first = jnp.where(at_lane, pltpu.roll(u, lane, 1) if lane else u, first)
                    last = jnp.where(at_lane, pltpu.roll(u, lane + 1, 1), last)
            pack[e, 0, eight(b), :] = first
            pack[e, 1, eight(b), :] = last
            return carry

        lax.fori_loop(0, 4, block, 0)

    def halo_copies(e, base, height):
        plan = []
        rows = pl.ds(base, height)
        plan.append((basis.at[pl.ds(21, 3), rows], row_in.at[e, 0, :, pl.ds(0, height)], (1, 0)))
        plan.append((basis.at[pl.ds(0, 3), rows], row_in.at[e, 1, :, pl.ds(0, height)], (-1, 0)))
        plan.append((pack.at[e, 1], col_in.at[e, 0], (0, 1)))
        plan.append((pack.at[e, 0], col_in.at[e, 1], (0, -1)))
        for k, (sx, sy) in enumerate(diagonals):
            plan.append((pack.at[e, 1 if sy < 0 else 0], diag_in.at[e, k], (-sx, -sy)))
        return [
            pltpu.make_async_remote_copy(
                src_ref=src,
                dst_ref=dst,
                send_sem=halo_send.at[e, k],
                recv_sem=halo_recv.at[e, k],
                device_id=peer(*to),
                device_id_type=MESH,
            )
            for k, (src, dst, to) in enumerate(plan)
        ]

    def apply(e, f, base, out_base):
        def block(b, carry):
            left, right = col_in[e, 0, eight(b), :], col_in[e, 1, eight(b), :]
            corners = [diag_in[e, k, eight(b), :] for k in range(4)]

            def three(x, c):
                if x < 0:
                    u = row_in[e, 0, c, eight(b, 32 * f), :]
                    lane, before, after = 32 * f + 21 + c, corners[0], corners[1]
                elif x > 7:
                    u = row_in[e, 1, c, eight(b, 32 * f), :]
                    lane, before, after = 32 * f + c, corners[2], corners[3]
                else:
                    u = basis[3 * x + c, eight(b, base), :]
                    lane, before, after = 32 * f + 3 * x + c, left, right
                before = pltpu.roll(before, 128 - lane, 1) if lane else before
                after = pltpu.roll(after, 127 - lane, 1)
                return {
                    0: u,
                    -1: jnp.where(lane8 == 0, before, pltpu.roll(u, 1, 1)),
                    1: jnp.where(lane8 == 127, after, pltpu.roll(u, 127, 1)),
                }

            window = {x: [three(x, c) for c in range(3)] for x in (-1, 0)}
            for x in range(8):
                window[x + 1] = [three(x + 1, c) for c in range(3)]
                field = [window[x][c][0] for c in range(3)]
                result = [coef[32 + c, x : x + 1, :] * field[c] for c in range(3)]
                for d, (dx, dy) in enumerate(offsets):
                    a = [coef[4 * d + c, x : x + 1, :] for c in range(3)]
                    soft = coef[4 * d + 3, x : x + 1, :]
                    stretch = [field[c] - window[x + dx][c][dy] for c in range(3)]
                    along = a[0] * stretch[0] + a[1] * stretch[1] + a[2] * stretch[2]
                    result = [result[c] + (a[c] * along + soft * stretch[c]) for c in range(3)]
                for c in range(3):
                    basis[3 * x + c, eight(b, out_base), :] = result[c]
            return carry

        lax.fori_loop(0, 4, block, 0)

    lane32, row32 = lanes(32), lax.broadcasted_iota(jnp.int32, (32, 128), 0)

    def local_sums(ref):
        total = jnp.zeros((96, 128), jnp.float32)
        cross = jnp.zeros((32, 128), jnp.float32)
        for q in range(0, 24, 2):
            rows = jnp.concatenate([ref[q, 0:128, :], ref[q + 1, 0:128, :]], 1)
            total = total + lax.dot_general(
                rows[:96],
                rows,
                (((1,), (1,)), ((), ())),
                precision=highest,
                preferred_element_type=jnp.float32,
            )
            for i in (q, q + 1):
                cross = cross + ref[i, SRCH : SRCH + 32, :] * ref[i, SIMG : SIMG + 32, :]
        cross = jnp.sum(cross, 1, keepdims=True)
        img_rows = total[64:96]
        top = jnp.where(lane32 < 96, total[0:32], img_rows)
        low = jnp.where(lane32 < 32, pltpu.roll(img_rows, 64, 1), total[32:64])
        low = jnp.where(lane32 == 96 + (row32 + 1) % 32, cross, low)
        return jnp.concatenate([top, low], 0)

    def sum_start(slots, n, me, axis, sweep, send, recv, value):
        slots[sweep, me] = value
        copies = []
        for o in range(1, n):
            copy = pltpu.make_async_remote_copy(
                src_ref=slots.at[sweep, me],
                dst_ref=slots.at[sweep, me],
                send_sem=send.at[sweep, o - 1],
                recv_sem=recv.at[sweep, o - 1],
                device_id=peer(o, 0) if axis == "x" else peer(0, o),
                device_id_type=MESH,
            )
            copy.start()
            copies.append(copy)
        return copies

    def sum_finish(slots, n, sweep, copies):
        for copy in copies:
            copy.wait_recv()
        total = slots[sweep, 0]
        for i in range(1, n):
            total = total + slots[sweep, i]
        return total

    sent = []

    def exchange(e, base, height):
        copies = halo_copies(e, base, height)
        for copy in copies:
            copy.start()
        sent.extend(copies)
        return copies

    pack_edges(0, (CUR, SRCH))
    pl.semaphore_wait(barrier, len(peers))
    first = exchange(0, CUR, 64)
    for copy in first:
        copy.wait_recv()
    apply(0, 0, CUR, IMG)
    pack_edges(1, (IMG,))
    second = exchange(1, IMG, 32)
    apply(0, 1, SRCH, SIMG)
    for copy in second:
        copy.wait_recv()
    apply(1, 0, IMG, IIMG)

    along_y = sum_start(slots_y, ny, gy, "y", 0, y_send, y_recv, local_sums(basis))
    sent.extend(along_y)
    pack_edges(2, (IIMG, SIMG))
    third = exchange(2, IIMG, 64)
    value = sum_finish(slots_y, ny, 0, along_y)
    along_x = sum_start(slots_x, nx, gx, "x", 0, x_send, x_recv, value)
    sent.extend(along_x)
    for copy in third:
        copy.wait_recv()
    apply(2, 0, IIMG, THIRD)
    apply(2, 1, SIMG, SIIMG)
    sums = sum_finish(slots_x, nx, 0, along_x) * (1.0 / entries)
    _, mixes, on_img, on_srch = small_step(sums[:32], sums[32:])

    def mixed(mix, ref, q, base):
        return jnp.dot(
            mix,
            jnp.concatenate([ref[q, base : base + 128, :], ref[q + 1, base : base + 128, :]], 1),
            precision=highest,
            preferred_element_type=jnp.float32,
        )

    for q in range(0, 24, 2):
        for mix, base, into in zip(mixes, (CUR, IMG, IIMG), (CUR, IMG, IIMG)):
            value = mixed(mix, basis, q, base)
            basis2[q, into : into + 32, :] = value[:, :128]
            basis2[q + 1, into : into + 32, :] = value[:, 128:]
        for i in (q, q + 1):
            for old_img, old, into in ((IMG, SRCH, SRCH), (IIMG, SIMG, SIMG)):
                basis2[i, into : into + 32, :] = (
                    on_img * basis[i, old_img : old_img + 32, :]
                    + on_srch * basis[i, old : old + 32, :]
                )

    along_y = sum_start(slots_y, ny, gy, "y", 1, y_send, y_recv, local_sums(basis2))
    sent.extend(along_y)
    value = sum_finish(slots_y, ny, 1, along_y)
    along_x = sum_start(slots_x, nx, gx, "x", 1, x_send, x_recv, value)
    sent.extend(along_x)
    sums = sum_finish(slots_x, nx, 1, along_x) * (1.0 / entries)
    lowest, mixes, _, _ = small_step(sums[:32], sums[32:])
    low_ref[...] = lowest
    for q in range(0, 24, 2):
        value = mixed(mixes[0], basis2, q, CUR)
        for i in (q, q + 1):
            x, c = i // 3, i % 3
            out_ref[pl.ds(8 * c + x, 32, stride=24), :] = value[:, 128 * (i - q) : 128 * (i - q) + 128]
    for copy in sent:
        copy.wait_send()


def solution(mesh):
    nx, ny = mesh.shape["gx"], mesh.shape["gy"]

    def body(modes_in, dirs_in, onsite, bond_terms, contacts):
        shape = modes_in.shape
        entries = float(3 * shape[2] * shape[3] * nx * ny)
        vmem = pl.BlockSpec(memory_space=pltpu.VMEM)
        f32 = jnp.float32
        modes, lowest = pl.pallas_call(
            functools.partial(kernel, nx, ny, entries),
            out_shape=(
                jax.ShapeDtypeStruct((768, 128), f32),
                jax.ShapeDtypeStruct((1, 128), f32),
            ),
            in_specs=[vmem] * 5,
            out_specs=(vmem, vmem),
            scratch_shapes=[
                pltpu.VMEM((24, 224, 128), f32),
                pltpu.VMEM((24, 160, 128), f32),
                pltpu.VMEM((35, 8, 128), f32),
                pltpu.VMEM((3, 2, 32, 128), f32),
                pltpu.VMEM((3, 2, 32, 128), f32),
                pltpu.VMEM((3, 4, 32, 128), f32),
                pltpu.VMEM((3, 2, 3, 64, 128), f32),
                pltpu.VMEM((2, ny, 64, 128), f32),
                pltpu.VMEM((2, nx, 64, 128), f32),
                pltpu.SemaphoreType.DMA((3, 8)),
                pltpu.SemaphoreType.DMA((3, 8)),
                pltpu.SemaphoreType.DMA((2, ny - 1)),
                pltpu.SemaphoreType.DMA((2, ny - 1)),
                pltpu.SemaphoreType.DMA((2, nx - 1)),
                pltpu.SemaphoreType.DMA((2, nx - 1)),
            ],
            compiler_params=pltpu.CompilerParams(
                collective_id=0, has_side_effects=True, vmem_limit_bytes=32 * 1024 * 1024
            ),
        )(
            modes_in.reshape(768, 128),
            dirs_in.reshape(768, 128),
            onsite,
            bond_terms,
            contacts,
        )
        return modes.reshape(shape), lowest[0, : shape[0]]

    in_specs = (
        P(None, None, ("pack", "gx"), "gy"),
        P(None, None, ("pack", "gx"), "gy"),
        P(None, ("pack", "gx"), "gy"),
        P(None, None, ("pack", "gx"), "gy"),
        P(None, ("pack", "gx"), "gy"),
    )
    out_specs = (P(None, None, ("pack", "gx"), "gy"), P("pack"))
    return jax.shard_map(body, mesh=mesh, in_specs=in_specs, out_specs=out_specs, check_vma=False)
```

time: 318 us -> 64.5 us (0.20)
  waiting for transfers between devices: 215 us -> 0 us
  Pallas kernels: 0 us -> 57.9 us
  other arithmetic: 32.9 us -> 0 us
  local copies, waits for them, and re-layouts: 25.3 us -> 5.61 us
  between operations: 15.4 us -> 0.65 us
  starting transfers between devices: 14.3 us -> 0 us
  matrix products: 14.2 us -> 0 us
    psum x2 -> x0, waiting for transfers between devices: 168 us -> none  [body(): lax.psum((jnp.dot(basis_rows, basis_rows.T, precision=highest), jnp.dot(b...]
    pallas_call x0 -> x1, Pallas kernels: none -> 57.9 us  [body(): pl.pallas_call(functools.partial(kernel, nx, ny, entries), out_shape=(jax...]
    ppermute x16 -> x0, waiting for transfers between devices: 47.5 us -> none  [the longest x8 27.1 us: with_halo(): lax.ppermute(head, axis, [((i + 1) % count, i) for i in range(count)])]
    ppermute x16 -> x0, starting transfers between devices: 14 us -> none  [the longest x8 8.86 us: with_halo(): lax.ppermute(head, axis, [((i + 1) % count, i) for i in range(count)])]
    another operation x16 -> x0, other arithmetic: 13.5 us -> none  [the longest x6 7.2 us: body(): chol_lower = jnp.linalg.cholesky(mode_gram)]
    dot_general x15 -> x0, matrix products: 13.1 us -> none  [the longest x2 3.4 us: body(): jnp.dot(basis_rows, basis_rows.T, precision=highest)]
    gather x8 -> x0, local copies, waits for them, and re-layouts: 7.07 us -> none  [diag_blocks(): jnp.diagonal(matrix.reshape(3, mode_count, 3, mode_count), axis1=1, axis2=3)]
    reshape x9 -> x0, local copies, waits for them, and re-layouts: 6.42 us -> none  [the longest x8 6.35 us: diag_blocks(): matrix.reshape(3, mode_count, 3, mode_count)]
  transfers between devices with their start and end apart: 18 -> 0, of which waited for: 17 -> 0; matrix products, arithmetic and copies ran while one was open for 2% -> 0% of each run, Pallas kernels for 0% -> 0%
where the time goes in v1:
time: 64.5 us; the launch traced here: 64.2 us
  Pallas kernels  57.9 us (90%)
  local copies, waits for them, and re-layouts  5.61 us (9%)
  between operations  0.65 us (1%)
    pallas_call x1, Pallas kernels, body(): pl.pallas_call(functools.partial(kernel, nx, ny, entries), out_shape=(jax...  57.9 us
    unnamed x11, local copies, waits for them, and re-layouts  5.1 us

profile of v1, /device:TPU:0, one launch (start us, length us, event | category | flops | bytes accessed | tf_op | source)
XLA Modules:
  0.0 64.2 jit_solution(2713269911857215560)
XLA Ops:
  0.6 0.0 copy-start
  0.6 1.0 %copy-done = f32[32,3,8,128]{3,2,1,0:T(8,128)S(1)} copy-done((f32[32,3,8,128]{3,2,1,0:T(8,128)S(1)}, f32[32,3,8,128]{3,2,1,0:T(8,128)}, u32[]{:S(2)}) %copy-start) | copy-done | bytes 393240
  1.6 0.0 copy-start.1
  1.6 1.0 %copy-done.1 = f32[32,3,8,128]{3,2,1,0:T(8,128)S(1)} copy-done((f32[32,3,8,128]{3,2,1,0:T(8,128)S(1)}, f32[32,3,8,128]{3,2,1,0:T(8,128)}, u32[]{:S(2)}) %copy-start.1) | copy-done | bytes 393240
  2.6 0.0 copy-start.2
  2.6 0.9 %copy-done.2 = f32[8,4,8,128]{3,2,1,0:T(8,128)S(1)} copy-done((f32[8,4,8,128]{3,2,1,0:T(8,128)S(1)}, f32[8,4,8,128]{3,2,1,0:T(8,128)}, u32[]{:S(2)}) %copy-start.2) | copy-done | bytes 131096
  3.5 0.0 copy-start.3
  3.5 0.8 %copy-done.3 = s32[8,8,128]{2,1,0:T(8,128)S(1)} copy-done((s32[8,8,128]{2,1,0:T(8,128)S(1)}, s32[8,8,128]{2,1,0:T(8,128)}, u32[]{:S(2)}) %copy-start.3) | copy-done | bytes 32792
  4.3 0.0 copy-start.4
  4.3 0.7 %copy-done.4 = f32[3,8,128]{2,1,0:T(8,128)S(1)} copy-done((f32[3,8,128]{2,1,0:T(8,128)S(1)}, f32[3,8,128]{2,1,0:T(8,128)}, u32[]{:S(2)}) %copy-start.4) | copy-done | bytes 12312
  5.0 57.9 %shard_map.68 = (f32[768,128]{1,0:T(8,128)S(1)}, f32[1,128]{1,0:T(1,128)S(1)}) custom-call(f32[768,128]{1,0:T(8,128)S(1)} %bitcast.6, f32[768,128]{1,0:T(8,128)S(1)} %bitcast.7, f32[3,8,128]{2,1,0:T(8,128)S(1)} %copy-done.4, f32[8,4,8,128]{3,2,1,0:T(8,128)S(1)} %copy-done.2, s32[8,8,128]{2,1,0:T(8,128)S(1)} %copy-done.3), custom_call_target="tpu_custom_call" | custom-call | tf_op jit(solution)/shard_map/pallas_call | solution.py:406
  62.9 0.5 slice_bitcast_fusion
  63.4 0.7 %copy.8 = f32[32,3,8,128]{3,2,1,0:T(8,128)} copy(f32[32,3,8,128]{3,2,1,0:T(8,128)S(1)} %bitcast.5) | data formatting | bytes 786432
Async XLA Ops:
  0.6 1.0 %copy-start = (f32[32,3,8,128]{3,2,1,0:T(8,128)S(1)}, f32[32,3,8,128]{3,2,1,0:T(8,128)}, u32[]{:S(2)}) copy-start(f32[32,3,8,128]{3,2,1,0:T(8,128)} %param.5) | copy-start | bytes 1179652
  1.6 1.0 %copy-start.1 = (f32[32,3,8,128]{3,2,1,0:T(8,128)S(1)}, f32[32,3,8,128]{3,2,1,0:T(8,128)}, u32[]{:S(2)}) copy-start(f32[32,3,8,128]{3,2,1,0:T(8,128)} %param.6) | copy-start | bytes 1179652
  2.6 0.9 %copy-start.2 = (f32[8,4,8,128]{3,2,1,0:T(8,128)S(1)}, f32[8,4,8,128]{3,2,1,0:T(8,128)}, u32[]{:S(2)}) copy-start(f32[8,4,8,128]{3,2,1,0:T(8,128)} %bond_ref.1) | copy-start | bytes 393220
  3.5 0.8 %copy-start.3 = (s32[8,8,128]{2,1,0:T(8,128)S(1)}, s32[8,8,128]{2,1,0:T(8,128)}, u32[]{:S(2)}) copy-start(s32[8,8,128]{2,1,0:T(8,128)} %contact_ref.1) | copy-start | bytes 98308
  4.3 0.7 %copy-start.4 = (f32[3,8,128]{2,1,0:T(8,128)S(1)}, f32[3,8,128]{2,1,0:T(8,128)}, u32[]{:S(2)}) copy-start(f32[3,8,128]{2,1,0:T(8,128)} %onsite_ref.1) | copy-start | bytes 36868

commit v2 on v1

--- a/solution.py
+++ b/solution.py
@@ -88,17 +88,23 @@
     aug = jnp.where(lane < 32, (lane == row).astype(jnp.float32), pltpu.roll(sym, 32, 1))
     blocks = [aug[8 * b : 8 * b + 8] for b in range(4)]
     sub = lax.broadcasted_iota(jnp.int32, (8, 128), 0)
-    for j in range(32):
-        home, at = j // 8, j % 8
-        pivot_row = blocks[home][at : at + 1]
-        scaled = pivot_row * (1.0 / pivot_row[:, 32 + j : 33 + j])
-        for b in range(home, 4):
-            if b == home and at == 7:
-                continue
-            step = blocks[b][:, 32 + j : 33 + j] * scaled
-            if b == home:
-                step = jnp.where(sub > at, step, 0.0)
-            blocks[b] = blocks[b] - step
+    for home in range(4):
+        cols = {
+            b: [
+                jnp.broadcast_to(blocks[b][:, 32 + 8 * home + i : 33 + 8 * home + i], (8, 128))
+                for i in range(8)
+            ]
+            for b in range(home, 4)
+        }
+        for i in range(8):
+            recip = 1.0 / cols[home][i][i : i + 1]
+            scaled = blocks[home][i : i + 1] * recip
+            ratios = {k: cols[home][k][i : i + 1] * recip for k in range(i + 1, 8)}
+            for b in range(home, 4):
+                factor = jnp.where(sub > i, cols[b][i], 0.0) if b == home else cols[b][i]
+                blocks[b] = blocks[b] - factor * scaled
+                for k, ratio in ratios.items():
+                    cols[b][k] = cols[b][k] - factor * ratio
     aug = jnp.concatenate(blocks, 0)
     pivots = jnp.sum(jnp.where(lane == row + 32, aug, 0.0), 1, keepdims=True)
     return jnp.where(lane < 32, aug / jnp.sqrt(pivots), 0.0)
@@ -146,13 +152,19 @@
     nx,
     ny,
     entries,
+    modes_hbm,
+    dirs_hbm,
+    onsite_hbm,
+    bond_hbm,
+    contact_hbm,
+    out_ref,
+    low_ref,
     modes_ref,
     dirs_ref,
     onsite_ref,
     bond_ref,
     contact_ref,
-    out_ref,
-    low_ref,
+    load_sem,
     basis,
     basis2,
     coef,
@@ -169,6 +181,16 @@
     x_send,
     x_recv,
 ):
+    held = (
+        (modes_hbm, modes_ref),
+        (dirs_hbm, dirs_ref),
+        (bond_hbm, bond_ref),
+        (contact_hbm, contact_ref),
+        (onsite_hbm, onsite_ref),
+    )
+    loads = [pltpu.make_async_copy(a, b, load_sem.at[i]) for i, (a, b) in enumerate(held)]
+    for load in loads:
+        load.start()
     part, gx, gy = lax.axis_index("pack"), lax.axis_index("gx"), lax.axis_index("gy")
 
     def peer(dx, dy):
@@ -186,39 +208,30 @@
     def eight(block, base=0):
         return pl.ds(pl.multiple_of(base + 8 * block, 8), 8)
 
-    for x in range(8):
-        for c in range(3):
-            basis[3 * x + c, CUR : CUR + 32] = modes_ref[pl.ds(8 * c + x, 32, stride=24), :]
-            basis[3 * x + c, SRCH : SRCH + 32] = dirs_ref[pl.ds(8 * c + x, 32, stride=24), :]
-    for d in range(8):
-        on = contact_ref[d].astype(jnp.float32)
-        for t in range(4):
-            coef[4 * d + t] = bond_ref[d, t] * on
-    for c in range(3):
-        coef[32 + c] = onsite_ref[c]
-
-    def pack_edges(e, fields):
-        def block(b, carry):
-            first = jnp.zeros((8, 128), jnp.float32)
-            last = jnp.zeros((8, 128), jnp.float32)
-            for f, base in enumerate(fields):
-                for q in range(24):
-                    lane = 32 * f + q
-                    u = basis[q, eight(b, base), :]
-                    at_lane = lane8 == lane
-                    first = jnp.where(at_lane, pltpu.roll(u, lane, 1) if lane else u, first)
-                    last = jnp.where(at_lane, pltpu.roll(u, lane + 1, 1), last)
-            pack[e, 0, eight(b), :] = first
-            pack[e, 1, eight(b), :] = last
-            return carry
-
-        lax.fori_loop(0, 4, block, 0)
-
-    def halo_copies(e, base, height):
+    def take(load, base, ref):
+        load.wait()
+        for x in range(8):
+            for c in range(3):
+                basis[3 * x + c, base : base + 32] = ref[pl.ds(8 * c + x, 32, stride=24), :]
+
+    def pack_edges(e, base):
+        first = jnp.zeros((8, 128), jnp.float32)
+        last = jnp.zeros((8, 128), jnp.float32)
+        for b in range(4):
+            for q in range(24):
+                lane = 32 * b + q
+                u = basis[q, base + 8 * b : base + 8 * b + 8, :]
+                at_lane = lane8 == lane
+                first = jnp.where(at_lane, pltpu.roll(u, lane, 1) if lane else u, first)
+                last = jnp.where(at_lane, pltpu.roll(u, lane + 1, 1), last)
+        pack[e, 0] = first
+        pack[e, 1] = last
+
+    def halo_copies(e, base):
         plan = []
-        rows = pl.ds(base, height)
-        plan.append((basis.at[pl.ds(21, 3), rows], row_in.at[e, 0, :, pl.ds(0, height)], (1, 0)))
-        plan.append((basis.at[pl.ds(0, 3), rows], row_in.at[e, 1, :, pl.ds(0, height)], (-1, 0)))
+        rows = pl.ds(base, 32)
+        plan.append((basis.at[pl.ds(21, 3), rows], row_in.at[e, 0], (1, 0)))
+        plan.append((basis.at[pl.ds(0, 3), rows], row_in.at[e, 1], (-1, 0)))
         plan.append((pack.at[e, 1], col_in.at[e, 0], (0, 1)))
         plan.append((pack.at[e, 0], col_in.at[e, 1], (0, -1)))
         for k, (sx, sy) in enumerate(diagonals):
@@ -235,21 +248,22 @@
             for k, (src, dst, to) in enumerate(plan)
         ]
 
-    def apply(e, f, base, out_base):
+    def apply(e, base, out_base):
         def block(b, carry):
-            left, right = col_in[e, 0, eight(b), :], col_in[e, 1, eight(b), :]
-            corners = [diag_in[e, k, eight(b), :] for k in range(4)]
+            shift = lax.rem(96 * b, 128)
+            left, right = (pltpu.roll(col_in[e, k], shift, 1) for k in range(2))
+            corners = [pltpu.roll(diag_in[e, k], shift, 1) for k in range(4)]
 
             def three(x, c):
                 if x < 0:
-                    u = row_in[e, 0, c, eight(b, 32 * f), :]
-                    lane, before, after = 32 * f + 21 + c, corners[0], corners[1]
+                    u = row_in[e, 0, c, eight(b), :]
+                    lane, before, after = 21 + c, corners[0], corners[1]
                 elif x > 7:
-                    u = row_in[e, 1, c, eight(b, 32 * f), :]
-                    lane, before, after = 32 * f + c, corners[2], corners[3]
+                    u = row_in[e, 1, c, eight(b), :]
+                    lane, before, after = c, corners[2], corners[3]
                 else:
                     u = basis[3 * x + c, eight(b, base), :]
-                    lane, before, after = 32 * f + 3 * x + c, left, right
+                    lane, before, after = 3 * x + c, left, right
                 before = pltpu.roll(before, 128 - lane, 1) if lane else before
                 after = pltpu.roll(after, 127 - lane, 1)
                 return {
@@ -324,37 +338,54 @@
 
     sent = []
 
-    def exchange(e, base, height):
-        copies = halo_copies(e, base, height)
+    def exchange(e, base):
+        copies = halo_copies(e, base)
         for copy in copies:
             copy.start()
         sent.extend(copies)
         return copies
 
-    pack_edges(0, (CUR, SRCH))
+    def arrived(copies):
+        for copy in copies:
+            copy.wait_recv()
+
+    take(loads[0], CUR, modes_ref)
+    pack_edges(0, CUR)
     pl.semaphore_wait(barrier, len(peers))
-    first = exchange(0, CUR, 64)
-    for copy in first:
-        copy.wait_recv()
-    apply(0, 0, CUR, IMG)
-    pack_edges(1, (IMG,))
-    second = exchange(1, IMG, 32)
-    apply(0, 1, SRCH, SIMG)
-    for copy in second:
-        copy.wait_recv()
-    apply(1, 0, IMG, IIMG)
+    of_cur = exchange(0, CUR)
+    take(loads[1], SRCH, dirs_ref)
+    pack_edges(1, SRCH)
+    of_srch = exchange(1, SRCH)
+    for load in loads[2:]:
+        load.wait()
+    for d in range(8):
+        on = contact_ref[d].astype(jnp.float32)
+        for t in range(4):
+            coef[4 * d + t] = bond_ref[d, t] * on
+    for c in range(3):
+        coef[32 + c] = onsite_ref[c]
+    arrived(of_cur)
+    apply(0, CUR, IMG)
+    pack_edges(2, IMG)
+    of_img = exchange(2, IMG)
+    arrived(of_srch)
+    apply(1, SRCH, SIMG)
+    pack_edges(3, SIMG)
+    arrived(of_img)
+    of_simg = exchange(3, SIMG)
+    apply(2, IMG, IIMG)
 
     along_y = sum_start(slots_y, ny, gy, "y", 0, y_send, y_recv, local_sums(basis))
     sent.extend(along_y)
-    pack_edges(2, (IIMG, SIMG))
-    third = exchange(2, IIMG, 64)
+    pack_edges(4, IIMG)
+    of_iimg = exchange(4, IIMG)
     value = sum_finish(slots_y, ny, 0, along_y)
     along_x = sum_start(slots_x, nx, gx, "x", 0, x_send, x_recv, value)
     sent.extend(along_x)
-    for copy in third:
-        copy.wait_recv()
-    apply(2, 0, IIMG, THIRD)
-    apply(2, 1, SIMG, SIIMG)
+    arrived(of_simg)
+    apply(3, SIMG, SIIMG)
+    arrived(of_iimg)
+    apply(4, IIMG, THIRD)
     sums = sum_finish(slots_x, nx, 0, along_x) * (1.0 / entries)
     _, mixes, on_img, on_srch = small_step(sums[:32], sums[32:])
 
@@ -409,27 +440,33 @@
                 jax.ShapeDtypeStruct((768, 128), f32),
                 jax.ShapeDtypeStruct((1, 128), f32),
             ),
-            in_specs=[vmem] * 5,
+            in_specs=[pl.BlockSpec(memory_space=pltpu.HBM)] * 5,
             out_specs=(vmem, vmem),
             scratch_shapes=[
+                pltpu.VMEM((768, 128), f32),
+                pltpu.VMEM((768, 128), f32),
+                pltpu.VMEM(onsite.shape, f32),
+                pltpu.VMEM(bond_terms.shape, f32),
+                pltpu.VMEM(contacts.shape, jnp.int32),
+                pltpu.SemaphoreType.DMA((5,)),
                 pltpu.VMEM((24, 224, 128), f32),
                 pltpu.VMEM((24, 160, 128), f32),
                 pltpu.VMEM((35, 8, 128), f32),
-                pltpu.VMEM((3, 2, 32, 128), f32),
-                pltpu.VMEM((3, 2, 32, 128), f32),
-                pltpu.VMEM((3, 4, 32, 128), f32),
-                pltpu.VMEM((3, 2, 3, 64, 128), f32),
+                pltpu.VMEM((5, 2, 8, 128), f32),
+                pltpu.VMEM((5, 2, 8, 128), f32),
+                pltpu.VMEM((5, 4, 8, 128), f32),
+                pltpu.VMEM((5, 2, 3, 32, 128), f32),
                 pltpu.VMEM((2, ny, 64, 128), f32),
                 pltpu.VMEM((2, nx, 64, 128), f32),
-                pltpu.SemaphoreType.DMA((3, 8)),
-                pltpu.SemaphoreType.DMA((3, 8)),
+                pltpu.SemaphoreType.DMA((5, 8)),
+                pltpu.SemaphoreType.DMA((5, 8)),
                 pltpu.SemaphoreType.DMA((2, ny - 1)),
                 pltpu.SemaphoreType.DMA((2, ny - 1)),
                 pltpu.SemaphoreType.DMA((2, nx - 1)),
                 pltpu.SemaphoreType.DMA((2, nx - 1)),
             ],
             compiler_params=pltpu.CompilerParams(
-                collective_id=0, has_side_effects=True, vmem_limit_bytes=32 * 1024 * 1024
+                collective_id=0, has_side_effects=True, vmem_limit_bytes=60 * 1024 * 1024
             ),
         )(
             modes_in.reshape(768, 128),

time: 64.5 us -> 52.7 us (0.82)
  Pallas kernels: 57.9 us -> 48.9 us
  local copies, waits for them, and re-layouts: 5.61 us -> 2.95 us
    pallas_call x1, Pallas kernels: 57.9 us -> 48.9 us  [body(): pl.pallas_call(functools.partial(kernel, nx, ny, entries), out_shape=(jax...]
    unnamed x11 -> x3, local copies, waits for them, and re-layouts: 5.1 us -> 2.44 us
where the time goes in v2:
time: 52.7 us; the launch traced here: 52.5 us
  Pallas kernels  48.9 us (93%)
  local copies, waits for them, and re-layouts  2.95 us (6%)
  between operations  0.65 us (1%)
    pallas_call x1, Pallas kernels, body(): pl.pallas_call(functools.partial(kernel, nx, ny, entries), out_shape=(jax...  48.9 us
    unnamed x3, local copies, waits for them, and re-layouts  2.44 us

profile of v2, /device:TPU:0, one launch (start us, length us, event | category | flops | bytes accessed | tf_op | source)
XLA Modules:
  0.0 52.5 jit_solution(3638447559302429982)
XLA Ops:
  0.6 48.9 %shard_map.68 = (f32[768,128]{1,0:T(8,128)}, f32[1,128]{1,0:T(1,128)}) custom-call(f32[768,128]{1,0:T(8,128)} %bitcast.6, f32[768,128]{1,0:T(8,128)} %bitcast.7, f32[3,8,128]{2,1,0:T(8,128)} %onsite_hbm.1, f32[8,4,8,128]{3,2,1,0:T(8,128)} %bond_hbm.1, s32[8,8,128]{2,1,0:T(8,128)} %contact_hbm.1), custom_call_target="tpu_custom_call" | custom-call | tf_op jit(solution)/shard_map/pallas_call | solution.py:437
  49.5 0.0 copy-start
  49.6 0.7 %copy-done = f32[1,128]{1,0:T(1,128)S(1)} copy-done((f32[1,128]{1,0:T(1,128)S(1)}, f32[1,128]{1,0:T(1,128)}, u32[]{:S(2)}) %copy-start) | copy-done | bytes 536
  50.2 0.5 slice_bitcast_fusion
  50.7 1.8 %copy.8 = f32[32,3,8,128]{3,2,1,0:T(8,128)} copy(f32[32,3,8,128]{3,2,1,0:T(8,128)} %bitcast.5) | data formatting | bytes 786432
Async XLA Ops:
  49.5 0.7 %copy-start = (f32[1,128]{1,0:T(1,128)S(1)}, f32[1,128]{1,0:T(1,128)}, u32[]{:S(2)}) copy-start(f32[1,128]{1,0:T(1,128)} %get-tuple-element.5) | copy-start | bytes 1540
